TPU v7x, 32 devices: a whole 2x2x4 slice. The times are simulated.
32 devices in a mesh: grp: 2 (over x), leaf: 16 (over z, y, core).
Axes of the slice: x: 2, y: 2, z: 4, core: 2. Of those that a mesh axis runs over, the one named last changes fastest.
Arguments:
- rhs: float32 [32, 256, 128], P(None, ('grp', 'leaf')), parts along dimension 1, may hold values from -6 to 6
- near_blocks: float32 [256, 8, 128, 128], P(('grp', 'leaf')), parts along dimension 0
- near_nbrs: int32 [256, 8], P(('grp', 'leaf')), parts along dimension 0, may hold values from 0 to 127, as said below
- row_basis: float32 [256, 128, 16], P(('grp', 'leaf')), parts along dimension 0, may hold values from -0.5 to 0.5
- col_basis: float32 [256, 128, 16], P(('grp', 'leaf')), parts along dimension 0, may hold values from -0.5 to 0.5
- couplings: float32 [4096, 16, 16], P(('grp', 'leaf')), parts along dimension 0, may hold values from -0.375 to 0.375
- far_owner: int32 [4096, 1], P(('grp', 'leaf')), parts along dimension 0, may hold values from 0 to 15; in each aligned block of 128 rows (0 to 127, 128 to 255, ...) at most 16 rows name the same one
- far_slot: int32 [4096], P(('grp', 'leaf')), parts along dimension 0, may hold values from 0 to 7
- leaf_perm: int32 [256, 128], P(('grp', 'leaf')), parts along dimension 0, may hold values from 0 to 127, each once within a row
- leaf_size: int32 [256], P(('grp', 'leaf')), parts along dimension 0, may hold values from 64 to 128, as said below
Outputs:
- solution: float32 [32, 256, 128], P(None, ('grp', 'leaf')), parts along dimension 1
There are 2 independent parts, one for each index of `grp`. A program takes and returns all parts, laid end to end along the dimension named above; each array names one. Nothing has to cross between parts.
Inputs may be any that keep to these rules, and one draw needn't show every extreme that they name: `near_nbrs`: entry 0 of a leaf's list is the leaf itself, entry 1 lies exactly 8 leaves away, and every entry lies within 8 leaves of the leaf. `far_owner`: among the far blocks of one device at most 16 name any one owner. `leaf_size`: the first leaf of every device is full.
All inputs are finite; a program needn't handle non-finite values.
Results may differ from a plain program's by a relative error of at most 0.0003.
Values sent between devices are 32-bit elements; how exact they have to be, the bound alone decides.
A program may use at most 64 MiB of HBM per device.

v0:
```python
import jax
import jax.numpy as jnp
from jax import lax
from jax.sharding import PartitionSpec as P

ITERS = 3


highest = lax.Precision.HIGHEST


def padded_2(shard, sides, width):
    for axis, dim in sides:
        peers, length = (lax.axis_size(axis), shard.shape[dim])
        up = [(i, (i + 1) % peers) for i in range(peers - 1)]
        down = [(j, i) for i, j in up]
        last = lax.slice_in_dim(shard, length - width, length, axis=dim)
        first = lax.slice_in_dim(shard, 0, width, axis=dim)
        before = lax.ppermute(last, axis, up)
        after = lax.ppermute(first, axis, down)
        shard = jnp.concatenate([before, shard, after], axis=dim)
    return shard


def inner_product(left_block, right_block):
    return jnp.einsum("rlm,slm->rs", left_block, right_block, precision=highest)


def cholesky_solve_block(gram_matrix, block_vector):
    factor = jnp.linalg.cholesky(gram_matrix)
    solved = jax.scipy.linalg.solve_triangular(
        factor, block_vector.reshape(block_vector.shape[0], -1), lower=True
    )
    return (factor, solved.reshape(block_vector.shape))


def shards(
    rhs,
    near_blocks,
    near_nbrs,
    row_basis,
    col_basis,
    couplings,
    far_owner,
    far_slot,
    leaf_perm,
    leaf_size,
):
    sides = rhs.shape[0]
    leaves_dev = rhs.shape[1]
    leaf_rows = rhs.shape[2]
    rank = col_basis.shape[2]
    far_dev = couplings.shape[0]
    far_leaf = far_dev // leaves_dev
    first_leaf = lax.axis_index("leaf") * leaves_dev
    positions = jnp.arange(leaf_rows, dtype=jnp.int32)
    live_mask = (positions[None, :] < leaf_size[:, None]).astype(jnp.float32)
    order = jnp.broadcast_to(leaf_perm[None], rhs.shape)
    start_block = jnp.take_along_axis(rhs, order, axis=2) * live_mask[None]
    window_index = near_nbrs - first_leaf + leaves_dev
    owners = far_owner[:, 0]
    columns = owners * leaves_dev + far_slot
    start_gram = lax.psum(inner_product(start_block, start_block), "leaf")
    first_factor, first_basis = cholesky_solve_block(start_gram, start_block)
    bases_list = [first_basis]
    hessenberg = jnp.zeros(((ITERS + 1) * sides, ITERS * sides), jnp.float32)
    for j in range(ITERS):
        field = bases_list[j]
        padded = padded_2(field, (("leaf", 1),), leaves_dev)
        picked = padded[:, window_index]
        near_part = jnp.einsum("rlnm,lnpm->rlp", picked, near_blocks, precision=highest)
        coefficients = jnp.einsum("rlm,lmk->lkr", field, col_basis, precision=highest).reshape(
            leaves_dev, rank * sides
        )
        portion = lax.all_gather(coefficients, "leaf", axis=0, tiled=True)
        inside = (columns >= 0) & (columns < portion.shape[0])
        chosen = portion[jnp.clip(columns, 0, portion.shape[0] - 1)]
        fetched = jnp.where(inside[:, None], chosen, 0.0)
        coupled = jnp.einsum(
            "bkj,bjr->bkr", couplings, fetched.reshape(far_dev, rank, sides), precision=highest
        )
        summed = coupled.reshape(leaves_dev, far_leaf, rank, sides).sum(axis=1)
        far_part = jnp.einsum("lpk,lkr->rlp", row_basis, summed, precision=highest)
        work_block = (near_part + far_part) * live_mask[None]
        for i in range(j + 1):
            projected = lax.psum(inner_product(bases_list[i], work_block), "leaf")
            hessenberg = hessenberg.at[
                i * sides : (i + 1) * sides, j * sides : (j + 1) * sides
            ].set(projected)
            work_block = work_block - jnp.einsum(
                "rs,rlm->slm", projected, bases_list[i], precision=highest
            )
        joined_gram = lax.psum(inner_product(work_block, work_block), "leaf")
        new_factor, new_basis = cholesky_solve_block(joined_gram, work_block)
        hessenberg = hessenberg.at[
            (j + 1) * sides : (j + 2) * sides, j * sides : (j + 1) * sides
        ].set(new_factor.T)
        bases_list.append(new_basis)
    target = jnp.zeros(((ITERS + 1) * sides, sides), jnp.float32).at[:sides].set(first_factor.T)
    normal_matrix = jnp.dot(hessenberg.T, hessenberg, precision=highest)
    small_side = jnp.dot(hessenberg.T, target, precision=highest)
    chol_factor = jnp.linalg.cholesky(normal_matrix)
    weights = jax.scipy.linalg.cho_solve((chol_factor, True), small_side)
    solution = jnp.zeros_like(start_block)
    for j in range(ITERS):
        solution = solution + jnp.einsum(
            "rs,rlm->slm", weights[j * sides : (j + 1) * sides], bases_list[j], precision=highest
        )
    return solution


def solution(mesh):
    in_specs = (
        P(None, ("grp", "leaf"), None),
        P(("grp", "leaf"), None, None, None),
        P(("grp", "leaf"), None),
        P(("grp", "leaf"), None, None),
        P(("grp", "leaf"), None, None),
        P(("grp", "leaf"), None, None),
        P(("grp", "leaf"), None),
        P(("grp", "leaf")),
        P(("grp", "leaf"), None),
        P(("grp", "leaf")),
    )
    out_specs = P(None, ("grp", "leaf"), None)
    return jax.shard_map(shards, mesh=mesh, in_specs=in_specs, out_specs=out_specs, check_vma=False)
```

profile of v0, /device:TPU:0, one launch (start us, length us, event | category | flops | bytes accessed | tf_op | source)
XLA Modules:
  0.0 946.3 jit_solution(7680030756193215662)
XLA Ops:
  2.3 190.9 %gather_fusion.6 = f32[32768]{0:T(1024)S(1)} fusion(f32[32,8,128]{2,1,0:T(8,128)S(1)} %copy-done, s32[32768]{0:T(1024)S(1)} %or_bitcast_fusion), kind=kCustom, calls=%fused_computation.6 | custom fusion | bytes 655360 | tf_op jit(solution)/shard_map/jit(take_along_axis)/gather | solution.py:59
  193.6 63.0 %psum.70 = f32[32,32]{0,1:T(8,128)S(1)} all-reduce(f32[32,32]{0,1:T(8,128)S(1)} %convolution_bitcast_fusion.18), channel_id=1, replica_groups=mesh['grp'=2,'leaf'=16] {'leaf'}, use_global_device_ids=true, to_apply=%region_0.0 | all-reduce | flops 1024 | bytes 8192 | tf_op jit(solution)/shard_map/psum | solution.py:63
  256.7 2.9 cholesky.109
  260.9 2.4 custom-call.20
  265.0 3.0 collective-permute-start
  268.6 17.8 %all_gather.9 = f32[128,512]{1,0:T(8,128)S(1)} all-gather(f32[8,512]{1,0:T(8,128)S(1)} %reshape.415), channel_id=1, replica_groups=mesh['grp'=2,'leaf'=16] {'leaf'}, dimensions={0}, use_global_device_ids=true | all-gather | bytes 278528 | tf_op jit(solution)/shard_map/all_gather | solution.py:75
  292.6 5.9 fusion.8
  298.8 59.6 %psum.71 = f32[32,32]{1,0:T(8,128)S(1)} all-reduce(f32[32,32]{1,0:T(8,128)S(1)} %convolution_bitcast_fusion.17), channel_id=1, replica_groups=mesh['grp'=2,'leaf'=16] {'leaf'}, use_global_device_ids=true, to_apply=%region_4.7 | all-reduce | flops 1024 | bytes 8192 | tf_op jit(solution)/shard_map/psum | solution.py:86
  359.0 57.6 %psum.72 = f32[32,32]{0,1:T(8,128)S(1)} all-reduce(f32[32,32]{0,1:T(8,128)S(1)} %convolution_bitcast_fusion.16), channel_id=1, replica_groups=mesh['grp'=2,'leaf'=16] {'leaf'}, use_global_device_ids=true, to_apply=%region_5.8 | all-reduce | flops 1024 | bytes 8192 | tf_op jit(solution)/shard_map/psum | solution.py:93
  416.7 2.9 cholesky.120
  420.9 2.4 custom-call.21
  425.4 3.0 collective-permute-start.2
  428.6 18.0 %all_gather.10 = f32[128,512]{1,0:T(8,128)S(1)} all-gather(f32[8,512]{1,0:T(8,128)S(1)} %reshape.419), channel_id=1, replica_groups=mesh['grp'=2,'leaf'=16] {'leaf'}, dimensions={0}, use_global_device_ids=true | all-gather | bytes 278528 | tf_op jit(solution)/shard_map/all_gather | solution.py:75
  450.9 5.9 fusion.6
  457.1 59.6 %psum.73 = f32[32,32]{1,0:T(8,128)S(1)} all-reduce(f32[32,32]{1,0:T(8,128)S(1)} %convolution_bitcast_fusion.15), channel_id=1, replica_groups=mesh['grp'=2,'leaf'=16] {'leaf'}, use_global_device_ids=true, to_apply=%region_8.11 | all-reduce | flops 1024 | bytes 8192 | tf_op jit(solution)/shard_map/psum | solution.py:86
  517.2 57.6 %psum.74 = f32[32,32]{1,0:T(8,128)S(1)} all-reduce(f32[32,32]{1,0:T(8,128)S(1)} %convolution_bitcast_fusion.14), channel_id=1, replica_groups=mesh['grp'=2,'leaf'=16] {'leaf'}, use_global_device_ids=true, to_apply=%region_9.12 | all-reduce | flops 1024 | bytes 8192 | tf_op jit(solution)/shard_map/psum | solution.py:86
  575.4 57.6 %psum.75 = f32[32,32]{0,1:T(8,128)S(1)} all-reduce(f32[32,32]{0,1:T(8,128)S(1)} %convolution_bitcast_fusion.13), channel_id=1, replica_groups=mesh['grp'=2,'leaf'=16] {'leaf'}, use_global_device_ids=true, to_apply=%region_10.13 | all-reduce | flops 1024 | bytes 8192 | tf_op jit(solution)/shard_map/psum | solution.py:93
  633.1 2.9 cholesky.131
  637.4 2.4 custom-call.22
  641.8 3.7 collective-permute-start.4
  645.5 2.0 dynamic-slice_select_fusion.1
  647.5 2.2 scatter.36
  650.7 18.1 %all_gather.11 = f32[128,512]{1,0:T(8,128)S(1)} all-gather(f32[8,512]{1,0:T(8,128)S(1)} %reshape.425), channel_id=1, replica_groups=mesh['grp'=2,'leaf'=16] {'leaf'}, dimensions={0}, use_global_device_ids=true | all-gather | bytes 278528 | tf_op jit(solution)/shard_map/all_gather | solution.py:75
  674.3 5.9 fusion.4
  680.5 59.6 %psum.76 = f32[32,32]{1,0:T(8,128)S(1)} all-reduce(f32[32,32]{1,0:T(8,128)S(1)} %convolution_bitcast_fusion.12), channel_id=1, replica_groups=mesh['grp'=2,'leaf'=16] {'leaf'}, use_global_device_ids=true, to_apply=%region_13.16 | all-reduce | flops 1024 | bytes 8192 | tf_op jit(solution)/shard_map/psum | solution.py:86
  742.3 2.2 scatter.41
  744.7 57.6 %psum.77 = f32[32,32]{1,0:T(8,128)S(1)} all-reduce(f32[32,32]{1,0:T(8,128)S(1)} %convolution_bitcast_fusion.11), channel_id=1, replica_groups=mesh['grp'=2,'leaf'=16] {'leaf'}, use_global_device_ids=true, to_apply=%region_14.17 | all-reduce | flops 1024 | bytes 8192 | tf_op jit(solution)/shard_map/psum | solution.py:86
  803.8 57.6 %psum.78 = f32[32,32]{1,0:T(8,128)S(1)} all-reduce(f32[32,32]{1,0:T(8,128)S(1)} %convolution_bitcast_fusion.10), channel_id=1, replica_groups=mesh['grp'=2,'leaf'=16] {'leaf'}, use_global_device_ids=true, to_apply=%region_15.18 | all-reduce | flops 1024 | bytes 8192 | tf_op jit(solution)/shard_map/psum | solution.py:86
  862.9 57.9 %psum.79 = f32[32,32]{0,1:T(8,128)S(1)} all-reduce(f32[32,32]{0,1:T(8,128)S(1)} %convolution_bitcast_fusion.9), channel_id=1, replica_groups=mesh['grp'=2,'leaf'=16] {'leaf'}, use_global_device_ids=true, to_apply=%region_16.19 | all-reduce | flops 1024 | bytes 8192 | tf_op jit(solution)/shard_map/psum | solution.py:93
  920.9 2.9 cholesky.142
  926.7 8.8 cholesky.41
  936.8 7.4 custom-call.15
  (144 shorter events, 43.8 us)
Async XLA Ops:
  0.0 2.2 copy-start
  2.2 191.0 %copy-start.6 = (s32[8]{0:T(128)S(1)}, s32[8]{0:T(128)}, u32[]{:S(2)}) copy-start(s32[8]{0:T(128)} %param.42) | copy-start | bytes 100
  2.2 191.1 %copy-start.4 = (s32[8,128]{1,0:T(8,128)S(1)}, s32[8,128]{1,0:T(8,128)}, u32[]{:S(2)}) copy-start(s32[8,128]{1,0:T(8,128)} %param.41) | copy-start | bytes 12292
  2.2 265.8 %copy-start.7 = (s32[128]{0:T(128)S(1)}, s32[128]{0:T(128)}, u32[]{:S(2)}) copy-start(s32[128]{0:T(128)} %param.40) | copy-start | bytes 1540
  2.3 265.8 %copy-start.8 = (s32[128,1]{0,1:T(1,128)S(1)}, s32[128,1]{0,1:T(1,128)}, u32[]{:S(2)}) copy-start(s32[128,1]{0,1:T(1,128)} %param.39) | copy-start | bytes 1540
  2.3 265.9 %copy-start.1 = (f32[8,128,16]{1,2,0:T(8,128)S(1)}, f32[8,128,16]{1,2,0:T(8,128)}, u32[]{:S(2)}) copy-start(f32[8,128,16]{1,2,0:T(8,128)} %param.37) | copy-start | bytes 196612
  193.2 94.7 %copy-start.3 = (f32[128,16,16]{0,2,1:T(8,128)S(1)}, f32[128,16,16]{0,2,1:T(8,128)}, u32[]{:S(2)}) copy-start(f32[128,16,16]{0,2,1:T(8,128)} %param.38) | copy-start | bytes 393220
  193.2 95.2 %copy-start.5 = (s32[8,8]{1,0:T(8,128)S(1)}, s32[8,8]{1,0:T(8,128)}, u32[]{:S(2)}) copy-start(s32[8,8]{1,0:T(8,128)} %param.35) | copy-start | bytes 772
  263.7 28.2 %collective-permute-start.1 = (f32[32,8,128]{2,0,1:T(8,128)S(1)}, f32[32,8,128]{2,0,1:T(8,128)S(1)}, u32[]{:S(2)}, u32[]{:S(2)}) collective-permute-start(f32[32,8,128]{2,0,1:T(8,128)S(1)} %bitcast.276), channel_id=1, source_target_pairs={{1,0},{2,1},{3,2},{4,3},{5,4},{6,5},{7,6},{8,7},{9,8},{10,9},{11,1... | collective-permute-start | bytes 393224 | tf_op jit(solution)/shard_map/ppermute | solution.py:20
  265.0 26.9 %collective-permute-start = (f32[32,8,128]{2,0,1:T(8,128)S(1)}, f32[32,8,128]{2,0,1:T(8,128)S(1)}, u32[]{:S(2)}, u32[]{:S(2)}) collective-permute-start(f32[32,8,128]{2,0,1:T(8,128)S(1)} %bitcast.277), channel_id=1, source_target_pairs={{0,1},{1,2},{2,3},{3,4},{4,5},{5,6},{6,7},{7,8},{8,9},{9,10},{10,1... | collective-permute-start | bytes 393224 | tf_op jit(solution)/shard_map/ppermute | solution.py:19
  268.6 22.2 %copy-start.2 = (f32[8,128,16]{1,2,0:T(8,128)S(1)}, f32[8,128,16]{1,2,0:T(8,128)}, u32[]{:S(2)}) copy-start(f32[8,128,16]{1,2,0:T(8,128)} %param.36) | copy-start | bytes 196612
  286.4 4.8 copy-start.9
  424.1 26.2 %collective-permute-start.3 = (f32[32,8,128]{2,0,1:T(8,128)S(1)}, f32[32,8,128]{2,0,1:T(8,128)S(1)}, u32[]{:S(2)}, u32[]{:S(2)}) collective-permute-start(f32[32,8,128]{2,0,1:T(8,128)S(1)} %bitcast.282), channel_id=1, source_target_pairs={{1,0},{2,1},{3,2},{4,3},{5,4},{6,5},{7,6},{8,7},{9,8},{10,9},{11,1... | collective-permute-start | bytes 393224 | tf_op jit(solution)/shard_map/ppermute | solution.py:20
  425.4 24.9 %collective-permute-start.2 = (f32[32,8,128]{2,0,1:T(8,128)S(1)}, f32[32,8,128]{2,0,1:T(8,128)S(1)}, u32[]{:S(2)}, u32[]{:S(2)}) collective-permute-start(f32[32,8,128]{2,0,1:T(8,128)S(1)} %bitcast.283), channel_id=1, source_target_pairs={{0,1},{1,2},{2,3},{3,4},{4,5},{5,6},{6,7},{7,8},{8,9},{9,10},{10,1... | collective-permute-start | bytes 393224 | tf_op jit(solution)/shard_map/ppermute | solution.py:19
  640.5 32.2 %collective-permute-start.5 = (f32[32,8,128]{2,0,1:T(8,128)S(1)}, f32[32,8,128]{2,0,1:T(8,128)S(1)}, u32[]{:S(2)}, u32[]{:S(2)}) collective-permute-start(f32[32,8,128]{2,0,1:T(8,128)S(1)} %bitcast.279), channel_id=1, source_target_pairs={{1,0},{2,1},{3,2},{4,3},{5,4},{6,5},{7,6},{8,7},{9,8},{10,9},{11,1... | collective-permute-start | bytes 393224 | tf_op jit(solution)/shard_map/ppermute | solution.py:20
  641.8 30.9 %collective-permute-start.4 = (f32[32,8,128]{2,0,1:T(8,128)S(1)}, f32[32,8,128]{2,0,1:T(8,128)}, u32[]{:S(2)}, u32[]{:S(2)}) collective-permute-start(f32[32,8,128]{2,0,1:T(8,128)S(1)} %bitcast.280), channel_id=1, source_target_pairs={{0,1},{1,2},{2,3},{3,4},{4,5},{5,6},{6,7},{7,8},{8,9},{9,10},{10,1... | collective-permute-start | bytes 393224 | tf_op jit(solution)/shard_map/ppermute | solution.py:19
where the time goes:
time: 947 us; the launch traced here: 946 us
  blocking collectives  642 us (68%)
  local copies, waits for them, and re-layouts  210 us (22%)
  other arithmetic  49.7 us (5%)
  matrix products  30.4 us (3%)
  starting transfers between devices  13.6 us (1%)
    psum x6, blocking collectives, shards(): projected = lax.psum(inner_product(bases_list[i], work_block), 'leaf')  352 us
    gather x2, local copies, waits for them, and re-layouts, shards(): start_block = jnp.take_along_axis(rhs, order, axis=2) * live_mask[None]  191 us
    psum x3, blocking collectives, shards(): joined_gram = lax.psum(inner_product(work_block, work_block), 'leaf')  173 us
    psum x1, blocking collectives, shards(): start_gram = lax.psum(inner_product(start_block, start_block), 'leaf')  63 us
    all_gather x3, blocking collectives, shards(): portion = lax.all_gather(coefficients, 'leaf', axis=0, tiled=True)  53.9 us
  transfers between devices with their start and end apart: 6, of which 0 were waited for; matrix products, arithmetic and copies ran while one was open for 2% of the time, Pallas kernels for 0%

commit v1 on v0

v1 whole, which is shorter than its diff:
```python
import functools

import jax
import jax.numpy as jnp
from jax import lax
from jax.experimental import pallas as pl
from jax.experimental.pallas import tpu as pltpu
from jax.sharding import PartitionSpec as P

F32 = jnp.float32
BF16 = jnp.bfloat16
HIGHEST = lax.Precision.HIGHEST
ITERS = 3
R = 32
M = 128
K = 16
NB = 8
LD = 8
CHUNK = 8
SPAN = 128 // CHUNK
NT = (((1,), (1,)), ((), ()))
NN = (((1,), (0,)), ((), ()))


def split(x):
    hi = x.astype(BF16)
    return hi, (x - hi.astype(F32)).astype(BF16)


def stacked(x):
    hi, lo = split(x)
    return jnp.concatenate([hi, lo], axis=0)


def dot(a, b, dims=NN, precision=None):
    return lax.dot_general(a, b, dims, precision=precision, preferred_element_type=F32)


def dot3(both, hi, lo, dims):
    rows = both.shape[0] // 2
    a = dot(both, hi, dims)
    return a[:rows] + a[rows:] + dot(both[:rows], lo, dims)


def kernel(
    n,
    near_hbm,
    kmat_hbm,
    nbr,
    size,
    rhs,
    perm,
    row_basis,
    col_basis,
    out,
    near_v,
    kmat_v,
    nh,
    nl,
    kh,
    kl,
    ch,
    cl,
    rh,
    rl,
    vs,
    wrecv,
    wsplit,
    crecv,
    gpart,
    grecv,
    gfull,
    mat,
    near_sem,
    kmat_sem,
    wsend,
    wsem,
    csend,
    csem,
    gsend,
    gsem,
    asend,
    asem,
):
    me = lax.axis_index("leaf")
    red = min(n, SPAN)

    loads = [pltpu.make_async_copy(near_hbm.at[l], near_v.at[l], near_sem.at[l]) for l in range(LD)]
    for load in loads:
        load.start()
    kload = pltpu.make_async_copy(kmat_hbm, kmat_v, kmat_sem)
    kload.start()

    barrier = pltpu.get_barrier_semaphore()

    def greet(k, carry):
        pl.semaphore_signal(
            barrier, inc=1, device_id={"leaf": lax.rem(me + k, n)}, device_id_type=pl.DeviceIdType.MESH
        )
        return carry

    lax.fori_loop(1, n, greet, 0)

    row_i = lax.broadcasted_iota(jnp.int32, (M, M), 0)
    col_i = lax.broadcasted_iota(jnp.int32, (M, M), 1)
    live = [
        lax.broadcasted_iota(jnp.int32, (R, M), 1) < size[l] for l in range(LD)
    ]

    for l in range(LD):
        x = rhs[:, l, :]
        hi, rest = split(x)
        rest = x - hi.astype(F32)
        mid, low = split(rest)
        pick = jnp.where((row_i == perm[l : l + 1, :]) & (col_i < size[l]), 1.0, 0.0).astype(BF16)
        parts = dot(jnp.concatenate([hi, mid, low], axis=0), pick)
        vs[l, 0:R, :] = (parts[0:R] + parts[R : 2 * R]) + parts[2 * R :]

    tile_k = lax.broadcasted_iota(jnp.int32, (K, M), 0)
    tile_c = lax.broadcasted_iota(jnp.int32, (K, M), 1)
    for l in range(LD):
        spread = jnp.where(tile_c == tile_k + l * K, 1.0, 0.0)
        hi, lo = split(dot(col_basis[l], spread, NN, HIGHEST))
        ch[l] = hi
        cl[l] = lo
        hi, lo = split(dot(row_basis[l], spread, NN, HIGHEST))
        rh[l] = hi
        rl[l] = lo

    pl.semaphore_wait(barrier, n - 1)

    def halo(step, to_right):
        side = 0 if to_right else 1
        return pltpu.make_async_remote_copy(
            src_ref=vs.at[:, pl.ds(step * R, R), :],
            dst_ref=wrecv.at[step, side],
            send_sem=wsend.at[step, side],
            recv_sem=wsem.at[step, side],
            device_id={"leaf": lax.rem(me + (1 if to_right else n - 1), n)},
            device_id_type=pl.DeviceIdType.MESH,
        )

    def coef(step, rows, target, source):
        return pltpu.make_async_remote_copy(
            src_ref=crecv.at[step, source, pl.ds(0, rows), :],
            dst_ref=crecv.at[step, source, pl.ds(0, rows), :],
            send_sem=csend.at[step, target],
            recv_sem=csem.at[step, source],
            device_id={"leaf": target},
            device_id_type=pl.DeviceIdType.MESH,
        )

    sigma = tau = None
    for step in range(ITERS):
        base = step * R
        rows = R + 8 if step == 0 else R

        @pl.when(me < n - 1)
        def _():
            halo(step, True).start()

        @pl.when(me > 0)
        def _():
            halo(step, False).start()

        coefs = jnp.zeros((R, M), F32)
        for l in range(LD):
            both = stacked(vs[l, base : base + R, :])
            wsplit[LD + l] = both
            coefs = coefs + dot3(both, ch[l], cl[l], NN)
        crecv[step, me, 0:R, :] = coefs

        if step == 0:
            trace = jnp.zeros((M, M), F32)
            power = jnp.zeros((M // 2, M), F32)
            count = jnp.zeros((1, M), F32)
            for l in range(LD):
                loads[l].wait()
                for s in range(NB):
                    x = near_v[l, s]
                    hi, lo = split(x)
                    nh[l, :, s * M : (s + 1) * M] = hi
                    nl[l, :, s * M : (s + 1) * M] = lo
                    power = power + x[: M // 2] * x[: M // 2]
                trace = trace + jnp.where((row_i == col_i) & (row_i < size[l]), near_v[l, 0], 0.0)
                count = count + jnp.where(col_i[:1] < size[l], 1.0, 0.0)
            power = jnp.where(col_i[: M // 2] < M // 2, power, 0.0)
            sums = [jnp.sum(jnp.sum(v, axis=0, keepdims=True), axis=1, keepdims=True) for v in (trace, power, count)]
            tile = lax.broadcasted_iota(jnp.int32, (8, M), 0)
            crecv[step, me, R : R + 8, :] = jnp.where(
                tile == 0, sums[0], jnp.where(tile == 1, sums[1], sums[2])
            )

        def send(k, carry):
            coef(step, rows, lax.rem(me + k, n), me).start()
            return carry

        lax.fori_loop(1, n, send, 0)

        if step == 0:
            kload.wait()
            hi, lo = split(kmat_v[...])
            kh[...] = hi
            kl[...] = lo

        for side in range(2):
            edge = (me > 0) if side == 0 else (me < n - 1)
            first = 0 if side == 0 else 2 * LD

            @pl.when(edge)
            def _():
                halo(step, side == 0).wait_recv()
                for l in range(LD):
                    wsplit[first + l] = stacked(wrecv[step, side, l])

            @pl.when(jnp.logical_not(edge))
            def _():
                for l in range(LD):
                    wsplit[first + l] = jnp.zeros((2 * R, M), BF16)

        near = []
        for l in range(LD):
            both = jnp.concatenate(
                [wsplit[jnp.clip(nbr[l, s] - me * LD + LD, 0, 3 * LD - 1)] for s in range(NB)], axis=1
            )
            near.append(dot3(both, nh[l], nl[l], NT))

        def arrive(k, carry):
            source = lax.rem(me + k, n)
            coef(step, rows, source, source).wait_recv()
            return carry

        lax.fori_loop(1, n, arrive, 0)

        if step == 0:
            total = crecv[0, 0, R : R + 8, :]
            for d in range(1, n):
                total = total + crecv[0, d, R : R + 8, :]
            sigma = total[0:1] / total[2:3]
            tau = jnp.sqrt(jnp.maximum(total[1:2] * (2.0 / (n * LD * (M // 2))), 1.0))

        z = jnp.zeros((R, M), F32)
        for d0 in range(0, n, 16):
            both = jnp.concatenate(
                [stacked(crecv[step, d, 0:R, :]) for d in range(d0, d0 + min(n, 16))], axis=1
            )
            rng = slice(d0 * M, (d0 + min(n, 16)) * M)
            z = z + dot3(both, kh[rng, :], kl[rng, :], NN)
        zz = stacked(z)
        for l in range(LD):
            w = near[l] + dot3(zz, rh[l], rl[l], NT)
            w = jnp.where(live[l], w, 0.0)
            vs[l, base + R : base + 2 * R, :] = (w - sigma * vs[l, base : base + R, :]) / tau

    gram = jnp.zeros((M, M), F32)
    for l in range(LD):
        gram = gram + dot(vs[l], vs[l], NT, HIGHEST)
    for i in range(SPAN):
        gpart[i] = gram[i * CHUNK : (i + 1) * CHUNK]

    def scatter(target, source):
        return pltpu.make_async_remote_copy(
            src_ref=gpart.at[target],
            dst_ref=grecv.at[source],
            send_sem=gsend.at[target],
            recv_sem=gsem.at[source],
            device_id={"leaf": target},
            device_id_type=pl.DeviceIdType.MESH,
        )

    def gather(target, source):
        return pltpu.make_async_remote_copy(
            src_ref=gfull.at[source],
            dst_ref=gfull.at[source],
            send_sem=asend.at[target],
            recv_sem=asem.at[source],
            device_id={"leaf": target},
            device_id_type=pl.DeviceIdType.MESH,
        )

    def when(condition, body):
        if n <= SPAN:
            body()
        else:
            pl.when(condition)(body)

    def over(body, wait):
        def one(k, carry):
            body(lax.rem(me + k, n))
            return carry

        lax.fori_loop(1, n, one, 0)

    over(lambda d: when(d < red, lambda: scatter(d, me).start()), False)

    def reduce():
        over(lambda d: scatter(me, d).wait_recv(), True)
        grecv[me] = gpart[me]
        total = grecv[0]
        for d in range(1, n):
            total = total + grecv[d]
        gfull[me] = total
        over(lambda d: gather(d, me).start(), False)

    when(me < red, reduce)
    over(lambda d: when(d < red, lambda: gather(me, d).wait_recv()), True)

    full = gfull[...].reshape(M, M)
    u = tau * full[R:] + sigma * full[: M - R]
    turned = pltpu.roll(u, M - R, axis=1)
    lane = lax.broadcasted_iota(jnp.int32, (M - R, M), 1)
    sub = lax.broadcasted_iota(jnp.int32, (M - R, M), 0)
    a = jnp.where(lane < M - R, tau * turned + sigma * u, turned)
    mat[0 : M - R, :] = a

    def eliminate(i, carry):
        a = mat[0 : M - R, :]
        line = mat[pl.ds(i, 1), :]
        column = jnp.sum(jnp.where(lane == i, a, 0.0), axis=1, keepdims=True)
        pivot = jnp.sum(jnp.where(lane[:1] == i, line, 0.0), axis=1, keepdims=True)
        line = line / pivot
        mat[0 : M - R, :] = jnp.where(sub == i, line, a - column * line)
        return carry

    lax.fori_loop(0, M - R, eliminate, 0)
    mat[M - R :, :] = jnp.zeros((R, M), F32)
    weights = mat[...].T[M - R :, :]
    for l in range(LD):
        out[:, l, :] = dot(weights, vs[l], NN, HIGHEST)

    for step in range(ITERS):

        @pl.when(me < n - 1)
        def _():
            halo(step, True).wait_send()

        @pl.when(me > 0)
        def _():
            halo(step, False).wait_send()

        rows = R + 8 if step == 0 else R
        over(lambda d: coef(step, rows, d, me).wait_send(), True)
    over(lambda d: when(d < red, lambda: scatter(d, me).wait_send()), True)
    when(me < red, lambda: over(lambda d: gather(d, me).wait_send(), True))


def shards(
    rhs,
    near_blocks,
    near_nbrs,
    row_basis,
    col_basis,
    couplings,
    far_owner,
    far_slot,
    leaf_perm,
    leaf_size,
):
    n = lax.axis_size("leaf")
    columns = (far_owner[:, 0] * LD + far_slot).reshape(LD, -1)
    far_leaf = columns.shape[1]
    chosen = (columns[:, :, None] == jnp.arange(n * LD, dtype=jnp.int32)).astype(F32)
    kmat = jnp.einsum(
        "lbj,lbkq->jqlk", chosen, couplings.reshape(LD, far_leaf, K, K), precision=HIGHEST
    ).reshape(n * M, M)
    vmem = pl.BlockSpec(memory_space=pltpu.VMEM)
    smem = pl.BlockSpec(memory_space=pltpu.SMEM)
    anyspace = pl.BlockSpec(memory_space=pl.ANY)
    dma = pltpu.SemaphoreType.DMA
    return pl.pallas_call(
        functools.partial(kernel, n),
        out_shape=jax.ShapeDtypeStruct((R, LD, M), F32),
        in_specs=[anyspace, anyspace, smem, smem, vmem, vmem, vmem, vmem],
        out_specs=vmem,
        scratch_shapes=[
            pltpu.VMEM((LD, NB, M, M), F32),
            pltpu.VMEM((n * M, M), F32),
            pltpu.VMEM((LD, M, NB * M), BF16),
            pltpu.VMEM((LD, M, NB * M), BF16),
            pltpu.VMEM((n * M, M), BF16),
            pltpu.VMEM((n * M, M), BF16),
            pltpu.VMEM((LD, M, M), BF16),
            pltpu.VMEM((LD, M, M), BF16),
            pltpu.VMEM((LD, M, M), BF16),
            pltpu.VMEM((LD, M, M), BF16),
            pltpu.VMEM((LD, M, M), F32),
            pltpu.VMEM((ITERS, 2, LD, R, M), F32),
            pltpu.VMEM((3 * LD, 2 * R, M), BF16),
            pltpu.VMEM((ITERS, n, R + 8, M), F32),
            pltpu.VMEM((SPAN, CHUNK, M), F32),
            pltpu.VMEM((n, CHUNK, M), F32),
            pltpu.VMEM((SPAN, CHUNK, M), F32),
            pltpu.VMEM((M, M), F32),
            dma((LD,)),
            dma,
            dma((ITERS, 2)),
            dma((ITERS, 2)),
            dma((ITERS, n)),
            dma((ITERS, n)),
            dma((n,)),
            dma((n,)),
            dma((n,)),
            dma((n,)),
        ],
        compiler_params=pltpu.CompilerParams(
            collective_id=0, has_side_effects=True, vmem_limit_bytes=48 * 1024 * 1024
        ),
    )(near_blocks, kmat, near_nbrs, leaf_size, rhs, leaf_perm, row_basis, col_basis)


def solution(mesh):
    in_specs = (
        P(None, ("grp", "leaf"), None),
        P(("grp", "leaf"), None, None, None),
        P(("grp", "leaf"), None),
        P(("grp", "leaf"), None, None),
        P(("grp", "leaf"), None, None),
        P(("grp", "leaf"), None, None),
        P(("grp", "leaf"), None),
        P(("grp", "leaf")),
        P(("grp", "leaf"), None),
        P(("grp", "leaf")),
    )
    out_specs = P(None, ("grp", "leaf"), None)
    return jax.shard_map(shards, mesh=mesh, in_specs=in_specs, out_specs=out_specs, check_vma=False)
```

time: 947 us -> 77.1 us (0.08)
  blocking collectives: 642 us -> 0 us
  local copies, waits for them, and re-layouts: 210 us -> 16.1 us
  Pallas kernels: 0 us -> 59.3 us
  other arithmetic: 49.7 us -> 0.68 us
  matrix products: 30.4 us -> 0.66 us
  starting transfers between devices: 13.6 us -> 0 us
    psum x10 -> x0, blocking collectives: 588 us -> none  [the longest x6 352 us: shards(): projected = lax.psum(inner_product(bases_list[i], work_block), 'leaf')]
    gather x11 -> x0, local copies, waits for them, and re-layouts: 195 us -> none  [the longest x2 191 us: shards(): start_block = jnp.take_along_axis(rhs, order, axis=2) * live_mask[None]]
    pallas_call x0 -> x1, Pallas kernels: none -> 59.3 us  [shards(): pl.pallas_call(functools.partial(kernel, n), out_shape=jax.ShapeDtypeStru...]
    all_gather x3 -> x0, blocking collectives: 53.9 us -> none  [shards(): portion = lax.all_gather(coefficients, 'leaf', axis=0, tiled=True)]
    another operation x29 -> x0, other arithmetic: 46.4 us -> none  [the longest x12 14.4 us: cholesky_solve_block(): factor = jnp.linalg.cholesky(gram_matrix)]
    dot_general x33 -> x0, matrix products: 28.9 us -> none  [the longest x3 17.8 us: shards(): jnp.einsum('rlnm,lnpm->rlp', picked, near_blocks, precision=highest)]
    ppermute x6 -> x0, starting transfers between devices: 13.6 us -> none  [the longest x3 9.75 us: padded_2(): before = lax.ppermute(last, axis, up)]
  transfers between devices with their start and end apart: 6 -> 0, of which waited for: 0 -> 0; matrix products, arithmetic and copies ran while one was open for 2% -> 0% of each run, Pallas kernels for 0% -> 0%
where the time goes in v1:
time: 77.1 us; the launch traced here: 76.9 us
  Pallas kernels  59.3 us (77%)
  local copies, waits for them, and re-layouts  16.1 us (21%)
    pallas_call x1, Pallas kernels, shards(): pl.pallas_call(functools.partial(kernel, n), out_shape=jax.ShapeDtypeStru...  59.3 us
    transpose x1, local copies, waits for them, and re-layouts, shards(): jnp.einsum('lbj,lbkq->jqlk', chosen, couplings.reshape(LD, far_leaf, K, K...  7.95 us
    reshape x1, local copies, waits for them, and re-layouts, shards(): kmat = jnp.einsum('lbj,lbkq->jqlk', chosen, couplings.reshape(LD, far_lea...  5.56 us

profile of v1, /device:TPU:0, one launch (start us, length us, event | category | flops | bytes accessed | tf_op | source)
XLA Modules:
  0.0 76.9 jit_solution(4811484015661930111)
XLA Ops:
  0.0 1.2 %reshape.9 = f32[8,16,16,16]{1,0,3,2:T(8,128)S(1)} reshape(f32[128,16,16]{0,2,1:T(8,128)} %param.15) | data formatting | bytes 262144 | tf_op jit(solution)/shard_map/reshape | solution.py:364
  1.2 0.2 copy.15
  1.4 0.7 bitcast_add_fusion
  2.1 0.1 eq.15
  2.2 0.7 fusion
  2.9 0.0 copy-start.4
  2.9 0.0 copy-start.5
  2.9 0.0 copy-start
  2.9 0.0 copy-start.1
  2.9 0.0 copy-start.2
  2.9 0.0 copy-start.3
  2.9 8.0 %copy.16 = f32[128,16,8,16]{3,2,1,0:T(8,128)} copy(f32[128,16,8,16]{0,1,3,2:T(8,128)S(1)} %bitcast.11) | data formatting | bytes 2097152 | tf_op jit(solution)/shard_map/lbj,lbkq->jqlk/transpose | solution.py:363
  10.9 5.6 %reshape.10.kmat_hbm = f32[2048,128]{1,0:T(8,128)S(1)} reshape(f32[128,16,8,16]{3,2,1,0:T(8,128)} %copy.16) | data formatting | bytes 2097152 | tf_op jit(solution)/shard_map/reshape | solution.py:365
  16.5 0.0 copy-done.4
  16.5 0.2 copy.17.row_basis
  16.7 0.0 copy-done.5
  16.7 0.2 copy.18.col_basis
  16.9 0.0 copy-done
  16.9 0.0 copy-done.1
  16.9 0.0 copy-done.2
  16.9 0.0 copy-done.3
  16.9 59.3 %shard_map.100 = f32[32,8,128]{2,1,0:T(8,128)S(1)} custom-call(f32[8,8,128,128]{3,2,1,0:T(8,128)} %near_hbm.1, f32[2048,128]{1,0:T(8,128)S(1)} %reshape.10.kmat_hbm, s32[8,8]{1,0:T(8,128)S(1)} %copy-done.1, s32[8]{0:T(128)S(1)} %copy-done.3, f32[32,8,128]{2,1,0:T(8,128)S(1)} %copy-done, s32[8,128]{1,0:T(8,128)S(1)} %copy-done.2, ...), custom_call_target="tpu_custom_call" | custom-call | tf_op jit(solution)/shard_map/pallas_call | solution.py:370
  76.3 0.7 copy.20
Async XLA Ops:
  2.9 13.6 %copy-start.4 = (f32[8,128,16]{1,2,0:T(8,128)S(1)}, f32[8,128,16]{1,2,0:T(8,128)}, u32[]{:S(2)}) copy-start(f32[8,128,16]{1,2,0:T(8,128)} %param.13) | copy-start | bytes 196612
  2.9 13.8 %copy-start.5 = (f32[8,128,16]{1,2,0:T(8,128)S(1)}, f32[8,128,16]{1,2,0:T(8,128)}, u32[]{:S(2)}) copy-start(f32[8,128,16]{1,2,0:T(8,128)} %param.14) | copy-start | bytes 196612
  2.9 14.0 %copy-start = (f32[32,8,128]{2,1,0:T(8,128)S(1)}, f32[32,8,128]{2,1,0:T(8,128)}, u32[]{:S(2)}) copy-start(f32[32,8,128]{2,1,0:T(8,128)} %rhs.1) | copy-start | bytes 393220
  2.9 14.0 %copy-start.1 = (s32[8,8]{1,0:T(8,128)S(1)}, s32[8,8]{1,0:T(8,128)}, u32[]{:S(2)}) copy-start(s32[8,8]{1,0:T(8,128)} %nbr.1) | copy-start | bytes 772
  2.9 14.0 %copy-start.2 = (s32[8,128]{1,0:T(8,128)S(1)}, s32[8,128]{1,0:T(8,128)}, u32[]{:S(2)}) copy-start(s32[8,128]{1,0:T(8,128)} %perm.1) | copy-start | bytes 12292
  2.9 14.0 %copy-start.3 = (s32[8]{0:T(128)S(1)}, s32[8]{0:T(128)}, u32[]{:S(2)}) copy-start(s32[8]{0:T(128)} %size.1) | copy-start | bytes 100

commit v2 on v1

--- a/solution.py
+++ b/solution.py
@@ -17,7 +17,8 @@
 NB = 8
 LD = 8
 CHUNK = 8
-SPAN = 128 // CHUNK
+PRE = 96
+SPAN = PRE // CHUNK
 NT = (((1,), (1,)), ((), ()))
 NN = (((1,), (0,)), ((), ()))
 
@@ -45,16 +46,26 @@
 def kernel(
     n,
     near_hbm,
-    kmat_hbm,
+    nbr_hbm,
+    size_hbm,
+    rhs_hbm,
+    perm_hbm,
+    row_hbm,
+    col_hbm,
+    cpl_hbm,
+    owner_hbm,
+    slot_hbm,
+    out,
     nbr,
     size,
     rhs,
     perm,
     row_basis,
     col_basis,
-    out,
+    cpl,
+    owner,
+    slot,
     near_v,
-    kmat_v,
     nh,
     nl,
     kh,
@@ -70,9 +81,10 @@
     gpart,
     grecv,
     gfull,
+    lrecv,
     mat,
+    small_sem,
     near_sem,
-    kmat_sem,
     wsend,
     wsem,
     csend,
@@ -81,15 +93,29 @@
     gsem,
     asend,
     asem,
+    lsend,
+    lsem,
 ):
     me = lax.axis_index("leaf")
-    red = min(n, SPAN)
-
+    red = PRE // CHUNK
+
+    pairs = (
+        (size_hbm, size),
+        (rhs_hbm, rhs),
+        (perm_hbm, perm),
+        (col_hbm, col_basis),
+        (row_hbm, row_basis),
+        (nbr_hbm, nbr),
+        (cpl_hbm, cpl),
+        (owner_hbm, owner),
+        (slot_hbm, slot),
+    )
+    smalls = [pltpu.make_async_copy(a, b, small_sem.at[i]) for i, (a, b) in enumerate(pairs)]
+    for load in smalls:
+        load.start()
     loads = [pltpu.make_async_copy(near_hbm.at[l], near_v.at[l], near_sem.at[l]) for l in range(LD)]
     for load in loads:
         load.start()
-    kload = pltpu.make_async_copy(kmat_hbm, kmat_v, kmat_sem)
-    kload.start()
 
     barrier = pltpu.get_barrier_semaphore()
 
@@ -100,6 +126,9 @@
         return carry
 
     lax.fori_loop(1, n, greet, 0)
+
+    for load in smalls:
+        load.wait()
 
     row_i = lax.broadcasted_iota(jnp.int32, (M, M), 0)
     col_i = lax.broadcasted_iota(jnp.int32, (M, M), 1)
@@ -116,14 +145,14 @@
         parts = dot(jnp.concatenate([hi, mid, low], axis=0), pick)
         vs[l, 0:R, :] = (parts[0:R] + parts[R : 2 * R]) + parts[2 * R :]
 
-    tile_k = lax.broadcasted_iota(jnp.int32, (K, M), 0)
-    tile_c = lax.broadcasted_iota(jnp.int32, (K, M), 1)
+    group = lax.broadcasted_iota(jnp.int32, (K, LD, M), 1)
     for l in range(LD):
-        spread = jnp.where(tile_c == tile_k + l * K, 1.0, 0.0)
-        hi, lo = split(dot(col_basis[l], spread, NN, HIGHEST))
+        wide = jnp.broadcast_to(col_basis[l][:, None, :], (K, LD, M))
+        hi, lo = split(jnp.where(group == l, wide, 0.0).reshape(M, M))
         ch[l] = hi
         cl[l] = lo
-        hi, lo = split(dot(row_basis[l], spread, NN, HIGHEST))
+        tall = jnp.concatenate([row_basis[l]] * LD, axis=0)
+        hi, lo = split(jnp.where(row_i // K == l, tall, 0.0))
         rh[l] = hi
         rl[l] = lo
 
@@ -150,6 +179,55 @@
             device_id_type=pl.DeviceIdType.MESH,
         )
 
+    def scatter(target, source):
+        return pltpu.make_async_remote_copy(
+            src_ref=gpart.at[target],
+            dst_ref=grecv.at[source],
+            send_sem=gsend.at[target],
+            recv_sem=gsem.at[source],
+            device_id={"leaf": target},
+            device_id_type=pl.DeviceIdType.MESH,
+        )
+
+    def gather(target, source):
+        return pltpu.make_async_remote_copy(
+            src_ref=gfull.at[source],
+            dst_ref=gfull.at[source],
+            send_sem=asend.at[target],
+            recv_sem=asem.at[source],
+            device_id={"leaf": target},
+            device_id_type=pl.DeviceIdType.MESH,
+        )
+
+    def final(target, source):
+        return pltpu.make_async_remote_copy(
+            src_ref=lrecv.at[source],
+            dst_ref=lrecv.at[source],
+            send_sem=lsend.at[target],
+            recv_sem=lsem.at[source],
+            device_id={"leaf": target},
+            device_id_type=pl.DeviceIdType.MESH,
+        )
+
+    def when(condition, body):
+        pl.when(condition)(body)
+
+    def over(body):
+        def one(k, carry):
+            body(lax.rem(me + k, n))
+            return carry
+
+        lax.fori_loop(1, n, one, 0)
+
+    def reduce():
+        over(lambda d: scatter(me, d).wait_recv())
+        grecv[me] = gpart[me]
+        total = grecv[0]
+        for d in range(1, n):
+            total = total + grecv[d]
+        gfull[me] = total
+        over(lambda d: gather(d, me).start())
+
     sigma = tau = None
     for step in range(ITERS):
         base = step * R
@@ -167,7 +245,7 @@
         for l in range(LD):
             both = stacked(vs[l, base : base + R, :])
             wsplit[LD + l] = both
-            coefs = coefs + dot3(both, ch[l], cl[l], NN)
+            coefs = coefs + dot3(both, ch[l], cl[l], NT)
         crecv[step, me, 0:R, :] = coefs
 
         if step == 0:
@@ -198,10 +276,29 @@
         lax.fori_loop(1, n, send, 0)
 
         if step == 0:
-            kload.wait()
-            hi, lo = split(kmat_v[...])
-            kh[...] = hi
-            kl[...] = lo
+            columns = owner[...] * LD + slot[...]
+            chosen = jnp.where(
+                lax.broadcasted_iota(jnp.int32, (n * LD, M), 0) == columns, 1.0, 0.0
+            ).astype(BF16)
+            far_leaf = M // LD
+            for k in range(0, K, 2):
+                both = []
+                for k2 in (k, k + 1):
+                    tall = jnp.concatenate([cpl[:, k2, :]] * LD, axis=0)
+                    hi, lo = split(jnp.where(row_i // K == col_i // far_leaf, tall, 0.0))
+                    both.append((dot(chosen, hi, NT) + dot(chosen, lo, NT)).reshape(n, LD, M))
+                hi, lo = split(jnp.concatenate(both, axis=1))
+                kh[:, k * LD : (k + 2) * LD, :] = hi
+                kl[:, k * LD : (k + 2) * LD, :] = lo
+
+        if step == ITERS - 1:
+            early = jnp.zeros((PRE, PRE), F32)
+            for l in range(LD):
+                early = early + dot(vs[l, 0:PRE, :], vs[l, 0:PRE, :], NT, HIGHEST)
+            early = jnp.concatenate([early, jnp.zeros((PRE, M - PRE), F32)], axis=1)
+            for i in range(SPAN):
+                gpart[i] = early[i * CHUNK : (i + 1) * CHUNK]
+            over(lambda d: when(d < red, lambda: scatter(d, me).start()))
 
         for side in range(2):
             edge = (me > 0) if side == 0 else (me < n - 1)
@@ -225,6 +322,9 @@
             )
             near.append(dot3(both, nh[l], nl[l], NT))
 
+        if step == ITERS - 1:
+            when(me < red, reduce)
+
         def arrive(k, carry):
             source = lax.rem(me + k, n)
             coef(step, rows, source, source).wait_recv()
@@ -244,85 +344,37 @@
             both = jnp.concatenate(
                 [stacked(crecv[step, d, 0:R, :]) for d in range(d0, d0 + min(n, 16))], axis=1
             )
-            rng = slice(d0 * M, (d0 + min(n, 16)) * M)
-            z = z + dot3(both, kh[rng, :], kl[rng, :], NN)
+            rng = slice(d0, d0 + min(n, 16))
+            z = z + dot3(both, kh[rng].reshape(-1, M), kl[rng].reshape(-1, M), NN)
         zz = stacked(z)
         for l in range(LD):
-            w = near[l] + dot3(zz, rh[l], rl[l], NT)
+            w = near[l] + dot3(zz, rh[l], rl[l], NN)
             w = jnp.where(live[l], w, 0.0)
             vs[l, base + R : base + 2 * R, :] = (w - sigma * vs[l, base : base + R, :]) / tau
 
-    gram = jnp.zeros((M, M), F32)
+    last = jnp.zeros((R, M), F32)
     for l in range(LD):
-        gram = gram + dot(vs[l], vs[l], NT, HIGHEST)
-    for i in range(SPAN):
-        gpart[i] = gram[i * CHUNK : (i + 1) * CHUNK]
-
-    def scatter(target, source):
-        return pltpu.make_async_remote_copy(
-            src_ref=gpart.at[target],
-            dst_ref=grecv.at[source],
-            send_sem=gsend.at[target],
-            recv_sem=gsem.at[source],
-            device_id={"leaf": target},
-            device_id_type=pl.DeviceIdType.MESH,
-        )
-
-    def gather(target, source):
-        return pltpu.make_async_remote_copy(
-            src_ref=gfull.at[source],
-            dst_ref=gfull.at[source],
-            send_sem=asend.at[target],
-            recv_sem=asem.at[source],
-            device_id={"leaf": target},
-            device_id_type=pl.DeviceIdType.MESH,
-        )
-
-    def when(condition, body):
-        if n <= SPAN:
-            body()
-        else:
-            pl.when(condition)(body)
-
-    def over(body, wait):
-        def one(k, carry):
-            body(lax.rem(me + k, n))
-            return carry
-
-        lax.fori_loop(1, n, one, 0)
-
-    over(lambda d: when(d < red, lambda: scatter(d, me).start()), False)
-
-    def reduce():
-        over(lambda d: scatter(me, d).wait_recv(), True)
-        grecv[me] = gpart[me]
-        total = grecv[0]
-        for d in range(1, n):
-            total = total + grecv[d]
-        gfull[me] = total
-        over(lambda d: gather(d, me).start(), False)
-
-    when(me < red, reduce)
-    over(lambda d: when(d < red, lambda: gather(me, d).wait_recv()), True)
-
-    full = gfull[...].reshape(M, M)
+        last = last + dot(vs[l, PRE:, :], vs[l], NT, HIGHEST)
+    lrecv[me] = last
+    over(lambda d: final(d, me).start())
+    over(lambda d: when(d < red, lambda: gather(me, d).wait_recv()))
+    over(lambda d: final(d, d).wait_recv())
+    last = lrecv[0]
+    for d in range(1, n):
+        last = last + lrecv[d]
+    first = gfull[...].reshape(PRE, M)
+    turned = jnp.concatenate([jnp.zeros((PRE, M), F32), last], axis=0).T
+    lane = lax.broadcasted_iota(jnp.int32, (PRE, M), 1)
+    sub = lax.broadcasted_iota(jnp.int32, (PRE, M), 0)
+    full = jnp.concatenate([jnp.where(lane < PRE, first, turned[:PRE]), last], axis=0)
     u = tau * full[R:] + sigma * full[: M - R]
     turned = pltpu.roll(u, M - R, axis=1)
-    lane = lax.broadcasted_iota(jnp.int32, (M - R, M), 1)
-    sub = lax.broadcasted_iota(jnp.int32, (M - R, M), 0)
     a = jnp.where(lane < M - R, tau * turned + sigma * u, turned)
-    mat[0 : M - R, :] = a
-
-    def eliminate(i, carry):
-        a = mat[0 : M - R, :]
-        line = mat[pl.ds(i, 1), :]
-        column = jnp.sum(jnp.where(lane == i, a, 0.0), axis=1, keepdims=True)
-        pivot = jnp.sum(jnp.where(lane[:1] == i, line, 0.0), axis=1, keepdims=True)
-        line = line / pivot
-        mat[0 : M - R, :] = jnp.where(sub == i, line, a - column * line)
-        return carry
-
-    lax.fori_loop(0, M - R, eliminate, 0)
+    for i in range(PRE):
+        line = a[i : i + 1, :]
+        line = line * (1.0 / line[:, i : i + 1])
+        a = jnp.where(sub == i, line, a - a[:, i : i + 1] * line)
+    mat[0:PRE, :] = a
     mat[M - R :, :] = jnp.zeros((R, M), F32)
     weights = mat[...].T[M - R :, :]
     for l in range(LD):
@@ -339,9 +391,10 @@
             halo(step, False).wait_send()
 
         rows = R + 8 if step == 0 else R
-        over(lambda d: coef(step, rows, d, me).wait_send(), True)
-    over(lambda d: when(d < red, lambda: scatter(d, me).wait_send()), True)
-    when(me < red, lambda: over(lambda d: gather(d, me).wait_send(), True))
+        over(lambda d: coef(step, rows, d, me).wait_send())
+    over(lambda d: when(d < red, lambda: scatter(d, me).wait_send()))
+    when(me < red, lambda: over(lambda d: gather(d, me).wait_send()))
+    over(lambda d: final(d, me).wait_send())
 
 
 def shards(
@@ -357,28 +410,29 @@
     leaf_size,
 ):
     n = lax.axis_size("leaf")
-    columns = (far_owner[:, 0] * LD + far_slot).reshape(LD, -1)
-    far_leaf = columns.shape[1]
-    chosen = (columns[:, :, None] == jnp.arange(n * LD, dtype=jnp.int32)).astype(F32)
-    kmat = jnp.einsum(
-        "lbj,lbkq->jqlk", chosen, couplings.reshape(LD, far_leaf, K, K), precision=HIGHEST
-    ).reshape(n * M, M)
     vmem = pl.BlockSpec(memory_space=pltpu.VMEM)
-    smem = pl.BlockSpec(memory_space=pltpu.SMEM)
-    anyspace = pl.BlockSpec(memory_space=pl.ANY)
+    anyspace = pl.BlockSpec(memory_space=pltpu.HBM)
     dma = pltpu.SemaphoreType.DMA
     return pl.pallas_call(
         functools.partial(kernel, n),
         out_shape=jax.ShapeDtypeStruct((R, LD, M), F32),
-        in_specs=[anyspace, anyspace, smem, smem, vmem, vmem, vmem, vmem],
+        in_specs=[anyspace] * 10,
         out_specs=vmem,
         scratch_shapes=[
+            pltpu.SMEM((LD, NB), jnp.int32),
+            pltpu.SMEM((LD,), jnp.int32),
+            pltpu.VMEM((R, LD, M), F32),
+            pltpu.VMEM((LD, M), jnp.int32),
+            pltpu.VMEM((LD, K, M), F32),
+            pltpu.VMEM((LD, K, M), F32),
+            pltpu.VMEM((K, K, M), F32),
+            pltpu.VMEM((1, M), jnp.int32),
+            pltpu.VMEM((1, M), jnp.int32),
             pltpu.VMEM((LD, NB, M, M), F32),
-            pltpu.VMEM((n * M, M), F32),
             pltpu.VMEM((LD, M, NB * M), BF16),
             pltpu.VMEM((LD, M, NB * M), BF16),
-            pltpu.VMEM((n * M, M), BF16),
-            pltpu.VMEM((n * M, M), BF16),
+            pltpu.VMEM((n, M, M), BF16),
+            pltpu.VMEM((n, M, M), BF16),
             pltpu.VMEM((LD, M, M), BF16),
             pltpu.VMEM((LD, M, M), BF16),
             pltpu.VMEM((LD, M, M), BF16),
@@ -390,9 +444,10 @@
             pltpu.VMEM((SPAN, CHUNK, M), F32),
             pltpu.VMEM((n, CHUNK, M), F32),
             pltpu.VMEM((SPAN, CHUNK, M), F32),
+            pltpu.VMEM((n, R, M), F32),
             pltpu.VMEM((M, M), F32),
+            dma((9,)),
             dma((LD,)),
-            dma,
             dma((ITERS, 2)),
             dma((ITERS, 2)),
             dma((ITERS, n)),
@@ -401,11 +456,24 @@
             dma((n,)),
             dma((n,)),
             dma((n,)),
+            dma((n,)),
+            dma((n,)),
         ],
         compiler_params=pltpu.CompilerParams(
-            collective_id=0, has_side_effects=True, vmem_limit_bytes=48 * 1024 * 1024
+            collective_id=0, has_side_effects=True, vmem_limit_bytes=56 * 1024 * 1024
         ),
-    )(near_blocks, kmat, near_nbrs, leaf_size, rhs, leaf_perm, row_basis, col_basis)
+    )(
+        near_blocks,
+        near_nbrs,
+        leaf_size,
+        rhs,
+        leaf_perm,
+        jnp.swapaxes(row_basis, 1, 2),
+        jnp.swapaxes(col_basis, 1, 2),
+        jnp.transpose(couplings, (1, 2, 0)),
+        far_owner.reshape(1, -1),
+        far_slot.reshape(1, -1),
+    )
 
 
 def solution(mesh):

time: 77.1 us -> 59 us (0.77)
  local copies, waits for them, and re-layouts: 16.1 us -> 1.57 us
  Pallas kernels: 59.3 us -> 57.2 us
    transpose x1 -> x0, local copies, waits for them, and re-layouts: 7.95 us -> none  [shards(): jnp.einsum('lbj,lbkq->jqlk', chosen, couplings.reshape(LD, far_leaf, K, K...]
    reshape x3 -> x0, local copies, waits for them, and re-layouts: 6.98 us -> none  [the longest x1 5.56 us: shards(): kmat = jnp.einsum('lbj,lbkq->jqlk', chosen, couplings.reshape(LD, far_lea...]
    pallas_call x1, Pallas kernels: 59.3 us -> 57.2 us  [shards(): pl.pallas_call(functools.partial(kernel, n), out_shape=jax.ShapeDtypeStru...]
    unnamed x15 -> x1, local copies, waits for them, and re-layouts: 1.08 us -> 1.57 us
where the time goes in v2:
time: 59 us; the launch traced here: 58.8 us
  Pallas kernels  57.2 us (97%)
  local copies, waits for them, and re-layouts  1.57 us (3%)
    pallas_call x1, Pallas kernels, shards(): pl.pallas_call(functools.partial(kernel, n), out_shape=jax.ShapeDtypeStru...  57.2 us
    unnamed x1, local copies, waits for them, and re-layouts  1.57 us

profile of v2, /device:TPU:0, one launch (start us, length us, event | category | flops | bytes accessed | tf_op | source)
XLA Modules:
  0.0 58.8 jit_solution(17380895377158067162)
XLA Ops:
  0.0 57.2 %shard_map.100 = f32[32,8,128]{2,1,0:T(8,128)} custom-call(f32[8,8,128,128]{3,2,1,0:T(8,128)} %near_hbm.1, s32[8,8]{1,0:T(8,128)} %nbr_hbm.1, s32[8]{0:T(128)} %size_hbm.1, f32[32,8,128]{2,1,0:T(8,128)} %rhs_hbm.1, s32[8,128]{1,0:T(8,128)} %perm_hbm.1, f32[8,16,128]{2,1,0:T(8,128)} %bitcast.6, f32[8,16,128]{2,1,0:T(8,128)} %bitcast.7, ...), custom_call_target="tpu_custom_call" | custom-call | tf_op jit(solution)/shard_map/pallas_call | solution.py:416
  57.2 1.6 %copy.12 = f32[32,8,128]{2,1,0:T(8,128)} copy(f32[32,8,128]{2,1,0:T(8,128)} %shard_map.100) | data formatting | bytes 262144

commit v3 on v2

--- a/solution.py
+++ b/solution.py
@@ -89,6 +89,7 @@
     wsem,
     csend,
     csem,
+    fsend,
     gsend,
     gsem,
     asend,
@@ -176,6 +177,18 @@
             send_sem=csend.at[step, target],
             recv_sem=csem.at[step, source],
             device_id={"leaf": target},
+            device_id_type=pl.DeviceIdType.MESH,
+        )
+
+    partner = me + 1 - 2 * lax.rem(me, 2)
+
+    def relay(step, rows, source):
+        return pltpu.make_async_remote_copy(
+            src_ref=crecv.at[step, source, pl.ds(0, rows), :],
+            dst_ref=crecv.at[step, source, pl.ds(0, rows), :],
+            send_sem=fsend.at[step, source],
+            recv_sem=csem.at[step, source],
+            device_id={"leaf": partner},
             device_id_type=pl.DeviceIdType.MESH,
         )
 
@@ -269,11 +282,13 @@
                 tile == 0, sums[0], jnp.where(tile == 1, sums[1], sums[2])
             )
 
+        coef(step, rows, partner, me).start()
+
         def send(k, carry):
-            coef(step, rows, lax.rem(me + k, n), me).start()
+            coef(step, rows, lax.rem(me + 2 * k, n), me).start()
             return carry
 
-        lax.fori_loop(1, n, send, 0)
+        lax.fori_loop(1, n // 2, send, 0)
 
         if step == 0:
             columns = owner[...] * LD + slot[...]
@@ -315,6 +330,14 @@
                 for l in range(LD):
                     wsplit[first + l] = jnp.zeros((2 * R, M), BF16)
 
+        def forward(k, carry):
+            source = lax.rem(me + 2 * k, n)
+            coef(step, rows, source, source).wait_recv()
+            relay(step, rows, source).start()
+            return carry
+
+        lax.fori_loop(1, n // 2, forward, 0)
+
         near = []
         for l in range(LD):
             both = jnp.concatenate(
@@ -326,11 +349,11 @@
             when(me < red, reduce)
 
         def arrive(k, carry):
-            source = lax.rem(me + k, n)
+            source = lax.rem(partner + 2 * k, n)
             coef(step, rows, source, source).wait_recv()
             return carry
 
-        lax.fori_loop(1, n, arrive, 0)
+        lax.fori_loop(0, n // 2, arrive, 0)
 
         if step == 0:
             total = crecv[0, 0, R : R + 8, :]
@@ -391,7 +414,15 @@
             halo(step, False).wait_send()
 
         rows = R + 8 if step == 0 else R
-        over(lambda d: coef(step, rows, d, me).wait_send())
+        coef(step, rows, partner, me).wait_send()
+
+        def sent(k, carry):
+            other = lax.rem(me + 2 * k, n)
+            coef(step, rows, other, me).wait_send()
+            relay(step, rows, other).wait_send()
+            return carry
+
+        lax.fori_loop(1, n // 2, sent, 0)
     over(lambda d: when(d < red, lambda: scatter(d, me).wait_send()))
     when(me < red, lambda: over(lambda d: gather(d, me).wait_send()))
     over(lambda d: final(d, me).wait_send())
@@ -452,6 +483,7 @@
             dma((ITERS, 2)),
             dma((ITERS, n)),
             dma((ITERS, n)),
+            dma((ITERS, n)),
             dma((n,)),
             dma((n,)),
             dma((n,)),

time: 59 us -> 55.2 us (0.936)
  Pallas kernels: 57.2 us -> 53.5 us
    pallas_call x1, Pallas kernels: 57.2 us -> 53.5 us  [shards(): pl.pallas_call(functools.partial(kernel, n), out_shape=jax.ShapeDtypeStru...]
where the time goes in v3:
time: 55.2 us; the launch traced here: 55.1 us
  Pallas kernels  53.5 us (97%)
  local copies, waits for them, and re-layouts  1.57 us (3%)
    pallas_call x1, Pallas kernels, shards(): pl.pallas_call(functools.partial(kernel, n), out_shape=jax.ShapeDtypeStru...  53.5 us
    unnamed x1, local copies, waits for them, and re-layouts  1.57 us

profile of v3, /device:TPU:0, one launch (start us, length us, event | category | flops | bytes accessed | tf_op | source)
XLA Modules:
  0.0 55.1 jit_solution(9247210000559214581)
XLA Ops:
  0.0 53.5 %shard_map.100 = f32[32,8,128]{2,1,0:T(8,128)} custom-call(f32[8,8,128,128]{3,2,1,0:T(8,128)} %near_hbm.1, s32[8,8]{1,0:T(8,128)} %nbr_hbm.1, s32[8]{0:T(128)} %size_hbm.1, f32[32,8,128]{2,1,0:T(8,128)} %rhs_hbm.1, s32[8,128]{1,0:T(8,128)} %perm_hbm.1, f32[8,16,128]{2,1,0:T(8,128)} %bitcast.6, f32[8,16,128]{2,1,0:T(8,128)} %bitcast.7, ...), custom_call_target="tpu_custom_call" | custom-call | tf_op jit(solution)/shard_map/pallas_call | solution.py:447
  53.5 1.6 %copy.12 = f32[32,8,128]{2,1,0:T(8,128)} copy(f32[32,8,128]{2,1,0:T(8,128)} %shard_map.100) | data formatting | bytes 262144
